TPU v7x, 256 devices: a whole 4x4x8 slice. The times are simulated.
256 devices in a mesh: blk: 256 (over y, x, z, core).
Axes of the slice: x: 4, y: 4, z: 8, core: 2. Of those that a mesh axis runs over, the one named last changes fastest.
Arguments:
- points: float32 [11, 524288], P(None, 'blk'), may hold values from -6 to 6
- values: float32 [16, 524288], P(None, 'blk'), may hold values from -0.046875 to 0.046875
- inverse_scale: float32 [11], replicated, may hold values from 0.08 to 0.4
Outputs:
- product: float32 [16, 524288], P(None, 'blk')
All inputs are finite; a program needn't handle non-finite values.
Results may differ from a plain program's by a relative error of at most 0.0003.
Values sent between devices are 32-bit elements; how exact they have to be, the bound alone decides.
A program may use at most 256 MiB of HBM per device.

v0:
```python
import functools
import math

import jax
import jax.numpy as jnp
from jax import lax
from jax.experimental import pallas as pl
from jax.experimental.pallas import tpu as pltpu
from jax.sharding import PartitionSpec as P

STEPS = 4
LN2 = math.log(2.0)
SHIFT = 1.5 / LN2
BUMP = 0.75 / LN2**2
FACTOR = LN2**2 / 3.0
POINT_SCALE = math.sqrt(5.0) / LN2
UP = 14
V8_MAX = 240.0
FIRST = 3
MESH = pl.DeviceIdType.MESH

bf16, f32, f8 = jnp.bfloat16, jnp.float32, jnp.float8_e4m3fn
T = 256
OWN_SLOT, NO_SLOT = 2, 3


def dot(a, b, transposed=False):
    dims = (((1,), (1 if transposed else 0,)), ((), ()))
    return lax.dot_general(a, b, dims, preferred_element_type=f32)


def matern(s):
    s = jnp.maximum(s, 1e-30)
    t = s * lax.rsqrt(s)
    y = t + SHIFT
    return (y * y + BUMP) * jnp.exp2(UP - t)


def parts3(x):
    high = x.astype(bf16).astype(f32)
    rest = x - high
    middle = rest.astype(bf16).astype(f32)
    return high, middle, rest - middle


def body(
    n,
    scale_ref, points_ref, values_ref, out_ref,
    send_buf, recv_buf, home_t, b_ref, v_ref, v8_ref,
    s_ref, kh0, kl0, kh1, kl1, oq, oq8, op, op8, ret_send, ret_recv,
    send_sem, recv_sem, rsend_sem, rrecv_sem,
):
    me = lax.axis_index("blk")
    feat, pts = points_ref.shape
    nc = pts // T
    own_steps = nc // 2 + 1
    total = own_steps + STEPS * nc
    high_refs, low_refs = (kh0, kh1), (kl0, kl1)

    def ahead(d):
        return lax.rem(me + d, n)

    def behind(d):
        return lax.rem(me + n - d, n)

    barrier = pltpu.get_barrier_semaphore()
    for d in range(1, STEPS + 1):
        pl.semaphore_signal(barrier, inc=1, device_id=(ahead(d),), device_id_type=MESH)
        pl.semaphore_signal(barrier, inc=1, device_id=(behind(d),), device_id_type=MESH)

    norm = jnp.zeros((1, pts), f32)
    for r in range(feat):
        w = points_ref[r : r + 1, :] * (scale_ref[r] * POINT_SCALE)
        send_buf[r : r + 1, :] = w
        norm = norm + w * w
    scaled = values_ref[...] * (FACTOR * 2.0**-UP)
    largest = jnp.max(jnp.max(jnp.abs(scaled), axis=0, keepdims=True), axis=1, keepdims=True)
    send_buf[feat : feat + 1, :] = norm
    send_buf[feat + 1 : feat + 2, :] = jnp.ones((1, pts), f32)
    send_buf[feat + 2 : feat + 3, :] = jnp.broadcast_to(
        jnp.maximum(largest, 1e-30) * (1.0 / V8_MAX), (1, pts)
    )
    send_buf[feat + 3 : 16, :] = jnp.zeros((13 - feat, pts), f32)
    send_buf[16:32, :] = scaled

    odd = lax.rem(me, 2)
    partner = me + 1 - 2 * odd

    def distance(k):
        return jnp.where(k == 0, 2, jnp.where(k == 1, 4, jnp.where(k == 2, 3, 1)))

    def block_copy(source, number, target, slot):
        return pltpu.make_async_remote_copy(
            src_ref=source,
            dst_ref=recv_buf.at[slot],
            send_sem=send_sem.at[number],
            recv_sem=recv_sem.at[slot],
            device_id=(target,),
            device_id_type=MESH,
        )

    def first_copy():
        return block_copy(send_buf, 0, behind(2), 0)

    def return_copy(k):
        return pltpu.make_async_remote_copy(
            src_ref=ret_send.at[k],
            dst_ref=ret_recv.at[distance(k) - 1],
            send_sem=rsend_sem.at[k],
            recv_sem=rrecv_sem.at[distance(k) - 1],
            device_id=(ahead(distance(k)),),
            device_id_type=MESH,
        )

    pl.semaphore_wait(barrier, 2 * STEPS)
    first_copy().start()

    @pl.when(odd == 1)
    def _():
        block_copy(send_buf, 3, partner, 3).start()

    def prepare(source, slot):
        for c in range(nc):
            cols = slice(c * T, (c + 1) * T)
            high, middle, low = (q.astype(bf16) for q in parts3(source[0:16, cols]))
            for g, part in enumerate((high, middle, high, middle, low, high)):
                b_ref[slot, 16 * g : 16 * g + 16, cols] = part
            v = source[16:32, cols]
            vh = v.astype(bf16)
            v_ref[slot, 0:16, cols] = vh
            v_ref[slot, 16:32, cols] = (v - vh.astype(f32)).astype(bf16)
            v8 = v * (1.0 / source[feat + 2 : feat + 3, cols])
            v8_ref[slot, :, cols] = jnp.concatenate([v8, jnp.zeros_like(v8)], 0).astype(f8)

    row = lax.broadcasted_iota(jnp.int32, (16, T), 0)
    nothing = jnp.zeros((32, T), f32)
    for c in range(nc):
        cols = slice(c * T, (c + 1) * T)
        y = jnp.where(
            row < feat,
            -2.0 * send_buf[0:16, cols],
            jnp.where(row == feat, 1.0, jnp.where(row == feat + 1, send_buf[feat : feat + 1, cols], 0.0)),
        )
        high, middle, low = parts3(y)
        left = jnp.concatenate([high, high, middle, middle, high, low, nothing], 0)
        home_t[cols, :] = left.T.astype(bf16)
    for slot in range(3):
        b_ref[slot, 96:128, :] = jnp.zeros((32, pts), bf16)
    prepare(send_buf, OWN_SLOT)
    for ref in (op, op8, oq, oq8):
        ref[...] = jnp.zeros_like(ref)

    def place(g):
        v = g - FIRST
        visit = jnp.logical_and(v >= 0, v < STEPS * nc)
        k = jnp.clip(v, 0, STEPS * nc - 1) // nc
        own = jnp.where(v < 0, g, g - STEPS * nc)
        slot = jnp.where(visit, lax.rem(k, 2), OWN_SLOT)
        offset = jnp.where(visit, jnp.clip(v, 0, STEPS * nc - 1) - k * nc, own)
        once = jnp.logical_or(own == 0, own == nc // 2)
        sums = jnp.where(visit, lax.rem(k, 2), jnp.where(once, NO_SLOT, OWN_SLOT))
        return slot, offset, sums

    def column(j, offset):
        return pl.ds(pl.multiple_of(lax.rem(j + offset, nc) * T, T), T)

    def cross(where, j):
        slot, offset, _ = where
        s_ref[:, j * T : (j + 1) * T] = dot(
            home_t[j * T : (j + 1) * T, :], b_ref[slot, :, column(j, offset)]
        )

    def elementwise(parity, j):
        for a in range(0, T, 32):
            rows, cols = slice(a, a + 32), slice(j * T, (j + 1) * T)
            k = matern(s_ref[rows, cols])
            high = k.astype(bf16)
            high_refs[parity][rows, cols] = high
            low_refs[parity][rows, cols] = (k - high.astype(f32)).astype(f8)

    def apply(where, parity, j):
        slot, offset, sums = where
        tile, cols = slice(j * T, (j + 1) * T), column(j, offset)
        kh, kl = high_refs[parity][:, tile], low_refs[parity][:, tile]
        op[:, tile] += dot(v_ref[slot, :, cols], kh, True)
        oq[sums, :, cols] += dot(v_ref[OWN_SLOT, :, tile], kh)
        op8[:, tile] += dot(v8_ref[slot, 0:16, cols], kl, True)
        oq8[sums, :, cols] += dot(v8_ref[OWN_SLOT, 0:16, tile], kl)

    def take(k):
        block_copy(send_buf, 0, partner, k).wait_recv()

        @pl.when(k == 0)
        def _():
            block_copy(recv_buf.at[0], 1, behind(2), 1).start()
            block_copy(recv_buf.at[0], 2, partner, 3 - odd).start()

        @pl.when(jnp.logical_and(k == 1, odd == 0))
        def _():
            block_copy(recv_buf.at[1], 3, partner, 2).start()

        prepare(recv_buf.at[k], lax.rem(k, 2))

    def settle(scale):
        op[0:16, :] += op8[...] * scale
        op8[...] = jnp.zeros_like(op8)

    def give_back(k):
        slot = lax.rem(k, 2)
        scale = send_buf[feat + 2 : feat + 3, :]
        ret_send[k] = oq[slot, 0:16, :] + oq[slot, 16:32, :] + oq8[slot] * scale
        return_copy(k).start()
        oq[slot] = jnp.zeros(oq.shape[1:], f32)
        oq8[slot] = jnp.zeros(oq8.shape[1:], f32)
        settle(recv_buf[k, feat + 2 : feat + 3, :])

    def events(g):
        due = g - FIRST + 1

        @pl.when(jnp.logical_and(lax.rem(due, nc) == 0, due < STEPS * nc))
        def _():
            take(due // nc)

        done = g - FIRST - 1

        @pl.when(done == 0)
        def _():
            settle(send_buf[feat + 2 : feat + 3, :])

        @pl.when(jnp.logical_and(lax.rem(done, nc) == 0, done > 0))
        def _():
            give_back(done // nc - 1)

    def work(g, parity):
        before, after = place(g - 1), place(jnp.minimum(g + 1, total - 1))
        for j in range(nc):
            elementwise(parity, j)
            cross(after, j)
            apply(before, 1 - parity, j)

    start, second = place(jnp.int32(0)), place(jnp.int32(1))
    for j in range(nc):
        cross(start, j)
    for j in range(nc):
        elementwise(0, j)
        cross(second, j)

    def pair(h, carry):
        g = 2 * h + 1
        work(g, 1)
        events(g + 1)
        work(g + 1, 0)
        return carry

    lax.fori_loop(0, (total - 1) // 2, pair, 0)
    final = place(jnp.int32(total - 1))
    for j in range(nc):
        apply(final, 0, j)

    for k in range(STEPS):
        block_copy(send_buf, k, partner, 0).wait_send()
        return_copy(k).wait_send()
        return_copy(k).wait_recv()
    for c in range(nc):
        cols = slice(c * T, (c + 1) * T)
        low = op8[:, cols] + oq8[OWN_SLOT, :, cols]
        sums = op[:, cols] + oq[OWN_SLOT, :, cols]
        result = sums[0:16] + sums[16:32] + low * send_buf[feat + 2 : feat + 3, cols]
        for k in range(STEPS):
            result = result + ret_recv[k, :, cols]
        out_ref[:, cols] = result


def per_device(n, points, values, inverse_scale):
    rhs, pts = values.shape
    vmem = pl.BlockSpec(memory_space=pltpu.VMEM)
    return pl.pallas_call(
        functools.partial(body, n),
        out_shape=jax.ShapeDtypeStruct((rhs, pts), f32),
        in_specs=[pl.BlockSpec(memory_space=pltpu.SMEM), vmem, vmem],
        out_specs=vmem,
        scratch_shapes=[
            pltpu.VMEM((32, pts), f32),
            pltpu.VMEM((STEPS, 32, pts), f32),
            pltpu.VMEM((pts, 128), bf16),
            pltpu.VMEM((3, 128, pts), bf16),
            pltpu.VMEM((3, 32, pts), bf16),
            pltpu.VMEM((3, 32, pts), f8),
            pltpu.VMEM((T, pts), f32),
            pltpu.VMEM((T, pts), bf16),
            pltpu.VMEM((T, pts), f8),
            pltpu.VMEM((T, pts), bf16),
            pltpu.VMEM((T, pts), f8),
            pltpu.VMEM((4, 32, pts), f32),
            pltpu.VMEM((4, 16, pts), f32),
            pltpu.VMEM((32, pts), f32),
            pltpu.VMEM((16, pts), f32),
            pltpu.VMEM((STEPS, rhs, pts), f32),
            pltpu.VMEM((STEPS, rhs, pts), f32),
            pltpu.SemaphoreType.DMA((STEPS,)),
            pltpu.SemaphoreType.DMA((STEPS,)),
            pltpu.SemaphoreType.DMA((STEPS,)),
            pltpu.SemaphoreType.DMA((STEPS,)),
        ],
        compiler_params=pltpu.CompilerParams(
            collective_id=0, has_side_effects=True, vmem_limit_bytes=48 << 20
        ),
        name="matern",
    )(inverse_scale, points, values)


def solution(mesh):
    placed = (P(None, "blk"), P(None, "blk"), P())
    return jax.shard_map(
        functools.partial(per_device, mesh.shape["blk"]),
        mesh=mesh, in_specs=placed, out_specs=P(None, "blk"), check_vma=False,
    )
```

profile of v0, /device:TPU:0, one launch (start us, length us, event | category | flops | bytes accessed | tf_op | source)
XLA Modules:
  0.0 66.6 jit_solution(6565456959137184376)
XLA Ops:
  0.0 0.0 copy-start
  0.0 0.9 %copy-done = f32[11,2048]{1,0:T(8,128)S(1)} copy-done((f32[11,2048]{1,0:T(8,128)S(1)}, f32[11,2048]{1,0:T(8,128)}, u32[]{:S(2)}) %copy-start) | copy-done | bytes 90136
  0.9 0.0 copy-start.1
  0.9 0.9 %copy-done.1 = f32[16,2048]{1,0:T(8,128)S(1)} copy-done((f32[16,2048]{1,0:T(8,128)S(1)}, f32[16,2048]{1,0:T(8,128)}, u32[]{:S(2)}) %copy-start.1) | copy-done | bytes 131096
  1.8 0.0 copy-start.2
  1.8 0.7 copy-done.2
  2.5 63.5 %matern.1 = f32[16,2048]{1,0:T(8,128)S(1)} custom-call(f32[11]{0:T(128)S(1)} %copy-done.2, f32[11,2048]{1,0:T(8,128)S(1)} %copy-done, f32[16,2048]{1,0:T(8,128)S(1)} %copy-done.1), custom_call_target="tpu_custom_call" | custom-call | tf_op jit(solution)/shard_map/matern/pallas_call | solution.py:277
  66.0 0.7 copy.5
Async XLA Ops:
  0.0 0.9 %copy-start = (f32[11,2048]{1,0:T(8,128)S(1)}, f32[11,2048]{1,0:T(8,128)}, u32[]{:S(2)}) copy-start(f32[11,2048]{1,0:T(8,128)} %points_ref.1) | copy-start | bytes 270340
  0.9 0.9 %copy-start.1 = (f32[16,2048]{1,0:T(8,128)S(1)}, f32[16,2048]{1,0:T(8,128)}, u32[]{:S(2)}) copy-start(f32[16,2048]{1,0:T(8,128)} %values_ref.1) | copy-start | bytes 393220
  1.8 0.7 copy-start.2
where the time goes:
time: 66.7 us; the launch traced here: 66.6 us
  Pallas kernels  63.5 us (95%)
  local copies, waits for them, and re-layouts  3.12 us (5%)
    pallas_call x1, Pallas kernels, per_device(): pl.pallas_call(functools.partial(body, n), out_shape=jax.ShapeDtypeStruct...  63.5 us
    unnamed x7, local copies, waits for them, and re-layouts  3.12 us

commit v1 on v0

--- a/solution.py
+++ b/solution.py
@@ -16,7 +16,6 @@
 POINT_SCALE = math.sqrt(5.0) / LN2
 UP = 14
 V8_MAX = 240.0
-FIRST = 3
 MESH = pl.DeviceIdType.MESH
 
 bf16, f32, f8 = jnp.bfloat16, jnp.float32, jnp.float8_e4m3fn
@@ -48,32 +47,42 @@
     scale_ref, points_ref, values_ref, out_ref,
     send_buf, recv_buf, home_t, b_ref, v_ref, v8_ref,
     s_ref, kh0, kl0, kh1, kl1, oq, oq8, op, op8, ret_send, ret_recv,
-    send_sem, recv_sem, rsend_sem, rrecv_sem,
+    points_buf, values_buf, send_sem, recv_sem, rsend_sem, rrecv_sem, load_sem,
 ):
     me = lax.axis_index("blk")
+    loads = [
+        pltpu.make_async_copy(points_ref, points_buf, load_sem.at[0]),
+        pltpu.make_async_copy(values_ref, values_buf, load_sem.at[1]),
+    ]
+    for load in loads:
+        load.start()
     feat, pts = points_ref.shape
     nc = pts // T
     own_steps = nc // 2 + 1
     total = own_steps + STEPS * nc
+    first = own_steps
     high_refs, low_refs = (kh0, kh1), (kl0, kl1)
 
     def ahead(d):
+        return lax.rem(me + n - d, n)
+
+    def behind(d):
         return lax.rem(me + d, n)
 
-    def behind(d):
-        return lax.rem(me + n - d, n)
-
+    odd = 1 - lax.rem(me, 2)
+    partner = me - 1 + 2 * odd
     barrier = pltpu.get_barrier_semaphore()
-    for d in range(1, STEPS + 1):
-        pl.semaphore_signal(barrier, inc=1, device_id=(ahead(d),), device_id_type=MESH)
-        pl.semaphore_signal(barrier, inc=1, device_id=(behind(d),), device_id_type=MESH)
-
+    for other in (ahead(2), partner):
+        pl.semaphore_signal(barrier, inc=1, device_id=(other,), device_id_type=MESH)
+
+    for load in loads:
+        load.wait()
     norm = jnp.zeros((1, pts), f32)
     for r in range(feat):
-        w = points_ref[r : r + 1, :] * (scale_ref[r] * POINT_SCALE)
+        w = points_buf[r : r + 1, :] * (scale_ref[r] * POINT_SCALE)
         send_buf[r : r + 1, :] = w
         norm = norm + w * w
-    scaled = values_ref[...] * (FACTOR * 2.0**-UP)
+    scaled = values_buf[...] * (FACTOR * 2.0**-UP)
     largest = jnp.max(jnp.max(jnp.abs(scaled), axis=0, keepdims=True), axis=1, keepdims=True)
     send_buf[feat : feat + 1, :] = norm
     send_buf[feat + 1 : feat + 2, :] = jnp.ones((1, pts), f32)
@@ -83,11 +92,11 @@
     send_buf[feat + 3 : 16, :] = jnp.zeros((13 - feat, pts), f32)
     send_buf[16:32, :] = scaled
 
-    odd = lax.rem(me, 2)
-    partner = me + 1 - 2 * odd
 
     def distance(k):
-        return jnp.where(k == 0, 2, jnp.where(k == 1, 4, jnp.where(k == 2, 3, 1)))
+        even_order = jnp.where(k == 0, 1, jnp.where(k == 1, 3, jnp.where(k == 2, 4, 2)))
+        odd_order = jnp.where(k == 0, 2, jnp.where(k == 1, 4, jnp.where(k == 2, 3, 1)))
+        return jnp.where(odd == 1, odd_order, even_order)
 
     def block_copy(source, number, target, slot):
         return pltpu.make_async_remote_copy(
@@ -100,7 +109,14 @@
         )
 
     def first_copy():
-        return block_copy(send_buf, 0, behind(2), 0)
+        return block_copy(send_buf, 0, behind(2), 3 - 3 * odd)
+
+    def relay(source):
+        block_copy(source, 1, behind(2), 2 - odd).start()
+        block_copy(source, 2, partner, 3 - 2 * odd).start()
+
+    def arrived(slot):
+        block_copy(send_buf, 0, partner, slot).wait_recv()
 
     def return_copy(k):
         return pltpu.make_async_remote_copy(
@@ -112,12 +128,12 @@
             device_id_type=MESH,
         )
 
-    pl.semaphore_wait(barrier, 2 * STEPS)
-    first_copy().start()
+    pl.semaphore_wait(barrier, 2)
 
     @pl.when(odd == 1)
     def _():
-        block_copy(send_buf, 3, partner, 3).start()
+        first_copy().start()
+        block_copy(send_buf, 3, partner, 0).start()
 
     def prepare(source, slot):
         for c in range(nc):
@@ -151,7 +167,7 @@
         ref[...] = jnp.zeros_like(ref)
 
     def place(g):
-        v = g - FIRST
+        v = g - first
         visit = jnp.logical_and(v >= 0, v < STEPS * nc)
         k = jnp.clip(v, 0, STEPS * nc - 1) // nc
         own = jnp.where(v < 0, g, g - STEPS * nc)
@@ -188,16 +204,13 @@
         oq8[sums, :, cols] += dot(v8_ref[OWN_SLOT, 0:16, tile], kl)
 
     def take(k):
-        block_copy(send_buf, 0, partner, k).wait_recv()
-
-        @pl.when(k == 0)
-        def _():
-            block_copy(recv_buf.at[0], 1, behind(2), 1).start()
-            block_copy(recv_buf.at[0], 2, partner, 3 - odd).start()
-
-        @pl.when(jnp.logical_and(k == 1, odd == 0))
-        def _():
-            block_copy(recv_buf.at[1], 3, partner, 2).start()
+        @pl.when(jnp.logical_or(odd == 1, k < 2))
+        def _():
+            arrived(k)
+
+        @pl.when(jnp.logical_and(odd == 1, k == 0))
+        def _():
+            relay(recv_buf.at[0])
 
         prepare(recv_buf.at[k], lax.rem(k, 2))
 
@@ -215,13 +228,27 @@
         settle(recv_buf[k, feat + 2 : feat + 3, :])
 
     def events(g):
-        due = g - FIRST + 1
-
-        @pl.when(jnp.logical_and(lax.rem(due, nc) == 0, due < STEPS * nc))
+        @pl.when(jnp.logical_and(g == 2, odd == 0))
+        def _():
+            first_copy().start()
+
+        due = g - first + 1
+
+        @pl.when(jnp.logical_and(lax.rem(due, nc) == 0, jnp.logical_and(due >= 0, due < STEPS * nc)))
         def _():
             take(due // nc)
 
-        done = g - FIRST - 1
+        @pl.when(jnp.logical_and(g == 6, odd == 0))
+        def _():
+            arrived(3)
+            relay(recv_buf.at[3])
+
+        @pl.when(jnp.logical_and(g == 14, odd == 0))
+        def _():
+            arrived(2)
+            block_copy(recv_buf.at[2], 3, partner, 2).start()
+
+        done = g - first - 1
 
         @pl.when(done == 0)
         def _():
@@ -244,7 +271,6 @@
     for j in range(nc):
         elementwise(0, j)
         cross(second, j)
-
     def pair(h, carry):
         g = 2 * h + 1
         work(g, 1)
@@ -256,6 +282,8 @@
     final = place(jnp.int32(total - 1))
     for j in range(nc):
         apply(final, 0, j)
+
+    give_back(STEPS - 1)
 
     for k in range(STEPS):
         block_copy(send_buf, k, partner, 0).wait_send()
@@ -277,7 +305,7 @@
     return pl.pallas_call(
         functools.partial(body, n),
         out_shape=jax.ShapeDtypeStruct((rhs, pts), f32),
-        in_specs=[pl.BlockSpec(memory_space=pltpu.SMEM), vmem, vmem],
+        in_specs=[pl.BlockSpec(memory_space=pltpu.SMEM)] + [pl.BlockSpec(memory_space=pl.ANY)] * 2,
         out_specs=vmem,
         scratch_shapes=[
             pltpu.VMEM((32, pts), f32),
@@ -297,10 +325,13 @@
             pltpu.VMEM((16, pts), f32),
             pltpu.VMEM((STEPS, rhs, pts), f32),
             pltpu.VMEM((STEPS, rhs, pts), f32),
+            pltpu.VMEM(points.shape, f32),
+            pltpu.VMEM(values.shape, f32),
             pltpu.SemaphoreType.DMA((STEPS,)),
             pltpu.SemaphoreType.DMA((STEPS,)),
             pltpu.SemaphoreType.DMA((STEPS,)),
             pltpu.SemaphoreType.DMA((STEPS,)),
+            pltpu.SemaphoreType.DMA((2,)),
         ],
         compiler_params=pltpu.CompilerParams(
             collective_id=0, has_side_effects=True, vmem_limit_bytes=48 << 20

time: 66.7 us -> 61.2 us (0.918)
  the two profiles are of different devices: /device:TPU:0 before, /device:TPU:1 now
where the time goes in v1:
time: 61.2 us; the launch traced here: 61.1 us
  Pallas kernels  58 us (95%)
  local copies, waits for them, and re-layouts  3.12 us (5%)
    pallas_call x1, Pallas kernels, per_device(): pl.pallas_call(functools.partial(body, n), out_shape=jax.ShapeDtypeStruct...  58 us
    unnamed x7, local copies, waits for them, and re-layouts  3.12 us

profile of v1, /device:TPU:1, one launch (start us, length us, event | category | flops | bytes accessed | tf_op | source)
XLA Modules:
  0.0 61.1 jit_solution(11772767486975099392)
XLA Ops:
  0.0 0.0 copy-start
  0.0 0.9 %copy-done = f32[11,2048]{1,0:T(8,128)S(1)} copy-done((f32[11,2048]{1,0:T(8,128)S(1)}, f32[11,2048]{1,0:T(8,128)}, u32[]{:S(2)}) %copy-start) | copy-done | bytes 90136
  0.9 0.0 copy-start.1
  0.9 0.9 %copy-done.1 = f32[16,2048]{1,0:T(8,128)S(1)} copy-done((f32[16,2048]{1,0:T(8,128)S(1)}, f32[16,2048]{1,0:T(8,128)}, u32[]{:S(2)}) %copy-start.1) | copy-done | bytes 131096
  1.8 0.0 copy-start.2
  1.8 0.7 %copy-done.2 = f32[11]{0:T(128)S(1)} copy-done((f32[11]{0:T(128)S(1)}, f32[11]{0:T(128)}, u32[]{:S(2)}) %copy-start.2) | copy-done | bytes 68
  2.5 58.0 %matern.1 = f32[16,2048]{1,0:T(8,128)S(1)} custom-call(f32[11]{0:T(128)S(1)} %copy-done.2, f32[11,2048]{1,0:T(8,128)S(1)} %copy-done, f32[16,2048]{1,0:T(8,128)S(1)} %copy-done.1), custom_call_target="tpu_custom_call" | custom-call | tf_op jit(solution)/shard_map/matern/pallas_call | solution.py:305
  60.5 0.7 %copy.5 = f32[16,2048]{1,0:T(8,128)} copy(f32[16,2048]{1,0:T(8,128)S(1)} %matern.1) | data formatting | bytes 262144
Async XLA Ops:
  0.0 0.9 %copy-start = (f32[11,2048]{1,0:T(8,128)S(1)}, f32[11,2048]{1,0:T(8,128)}, u32[]{:S(2)}) copy-start(f32[11,2048]{1,0:T(8,128)} %points_ref.1) | copy-start | bytes 270340
  0.9 0.9 %copy-start.1 = (f32[16,2048]{1,0:T(8,128)S(1)}, f32[16,2048]{1,0:T(8,128)}, u32[]{:S(2)}) copy-start(f32[16,2048]{1,0:T(8,128)} %values_ref.1) | copy-start | bytes 393220
  1.8 0.7 %copy-start.2 = (f32[11]{0:T(128)S(1)}, f32[11]{0:T(128)}, u32[]{:S(2)}) copy-start(f32[11]{0:T(128)} %scale_ref.1) | copy-start | bytes 136

commit v2 on v1

--- a/solution.py
+++ b/solution.py
@@ -44,15 +44,16 @@
 
 def body(
     n,
-    scale_ref, points_ref, values_ref, out_ref,
+    scale_hbm, points_ref, values_ref, out_ref,
     send_buf, recv_buf, home_t, b_ref, v_ref, v8_ref,
     s_ref, kh0, kl0, kh1, kl1, oq, oq8, op, op8, ret_send, ret_recv,
-    points_buf, values_buf, send_sem, recv_sem, rsend_sem, rrecv_sem, load_sem,
+    points_buf, values_buf, scale_ref, send_sem, recv_sem, rsend_sem, rrecv_sem, load_sem,
 ):
     me = lax.axis_index("blk")
     loads = [
         pltpu.make_async_copy(points_ref, points_buf, load_sem.at[0]),
         pltpu.make_async_copy(values_ref, values_buf, load_sem.at[1]),
+        pltpu.make_async_copy(scale_hbm, scale_ref, load_sem.at[2]),
     ]
     for load in loads:
         load.start()
@@ -238,12 +239,12 @@
         def _():
             take(due // nc)
 
-        @pl.when(jnp.logical_and(g == 6, odd == 0))
+        @pl.when(jnp.logical_and(g == 10, odd == 0))
         def _():
             arrived(3)
             relay(recv_buf.at[3])
 
-        @pl.when(jnp.logical_and(g == 14, odd == 0))
+        @pl.when(jnp.logical_and(g == 18, odd == 0))
         def _():
             arrived(2)
             block_copy(recv_buf.at[2], 3, partner, 2).start()
@@ -305,7 +306,7 @@
     return pl.pallas_call(
         functools.partial(body, n),
         out_shape=jax.ShapeDtypeStruct((rhs, pts), f32),
-        in_specs=[pl.BlockSpec(memory_space=pltpu.SMEM)] + [pl.BlockSpec(memory_space=pl.ANY)] * 2,
+        in_specs=[pl.BlockSpec(memory_space=pltpu.HBM)] * 3,
         out_specs=vmem,
         scratch_shapes=[
             pltpu.VMEM((32, pts), f32),
@@ -327,14 +328,15 @@
             pltpu.VMEM((STEPS, rhs, pts), f32),
             pltpu.VMEM(points.shape, f32),
             pltpu.VMEM(values.shape, f32),
+            pltpu.SMEM(inverse_scale.shape, f32),
             pltpu.SemaphoreType.DMA((STEPS,)),
             pltpu.SemaphoreType.DMA((STEPS,)),
             pltpu.SemaphoreType.DMA((STEPS,)),
             pltpu.SemaphoreType.DMA((STEPS,)),
-            pltpu.SemaphoreType.DMA((2,)),
+            pltpu.SemaphoreType.DMA((3,)),
         ],
         compiler_params=pltpu.CompilerParams(
-            collective_id=0, has_side_effects=True, vmem_limit_bytes=48 << 20
+            collective_id=0, has_side_effects=True, vmem_limit_bytes=63 << 20
         ),
         name="matern",
     )(inverse_scale, points, values)

time: 61.2 us -> 61.2 us (level)
  local copies, waits for them, and re-layouts: 3.12 us -> 1.57 us
  Pallas kernels: 58 us -> 59.5 us
    unnamed x7 -> x1, local copies, waits for them, and re-layouts: 3.12 us -> 1.57 us
    pallas_call x1, Pallas kernels: 58 us -> 59.5 us  [per_device(): pl.pallas_call(functools.partial(body, n), out_shape=jax.ShapeDtypeStruct...]
where the time goes in v2:
time: 61.2 us; the launch traced here: 61.1 us
  Pallas kernels  59.5 us (97%)
  local copies, waits for them, and re-layouts  1.57 us (3%)
    pallas_call x1, Pallas kernels, per_device(): pl.pallas_call(functools.partial(body, n), out_shape=jax.ShapeDtypeStruct...  59.5 us
    unnamed x1, local copies, waits for them, and re-layouts  1.57 us

profile of v2, /device:TPU:1, one launch (start us, length us, event | category | flops | bytes accessed | tf_op | source)
XLA Modules:
  0.0 61.1 jit_solution(11281622680260761657)
XLA Ops:
  0.0 59.5 %matern.1 = f32[16,2048]{1,0:T(8,128)} custom-call(f32[11]{0:T(128)} %scale_hbm.1, f32[11,2048]{1,0:T(8,128)} %points_ref.1, f32[16,2048]{1,0:T(8,128)} %values_ref.1), custom_call_target="tpu_custom_call" | custom-call | tf_op jit(solution)/shard_map/matern/pallas_call | solution.py:306
  59.5 1.6 %copy.5 = f32[16,2048]{1,0:T(8,128)} copy(f32[16,2048]{1,0:T(8,128)} %matern.1) | data formatting | bytes 262144

commit v3 on v2

--- a/solution.py
+++ b/solution.py
@@ -239,12 +239,12 @@
         def _():
             take(due // nc)
 
-        @pl.when(jnp.logical_and(g == 10, odd == 0))
+        @pl.when(jnp.logical_and(g == 6, odd == 0))
         def _():
             arrived(3)
             relay(recv_buf.at[3])
 
-        @pl.when(jnp.logical_and(g == 18, odd == 0))
+        @pl.when(jnp.logical_and(g == 14, odd == 0))
         def _():
             arrived(2)
             block_copy(recv_buf.at[2], 3, partner, 2).start()

time: 61.2 us -> 61.2 us (level)
  no operation moved by 1% of the time
where the time goes in v3:
time: 61.2 us; the launch traced here: 61.1 us
  Pallas kernels  59.5 us (97%)
  local copies, waits for them, and re-layouts  1.57 us (3%)
    pallas_call x1, Pallas kernels, per_device(): pl.pallas_call(functools.partial(body, n), out_shape=jax.ShapeDtypeStruct...  59.5 us
    unnamed x1, local copies, waits for them, and re-layouts  1.57 us

profile of v3, /device:TPU:1, one launch (start us, length us, event | category | flops | bytes accessed | tf_op | source)
XLA Modules:
  0.0 61.1 jit_solution(12324754784077662163)
XLA Ops:
  0.0 59.5 %matern.1 = f32[16,2048]{1,0:T(8,128)} custom-call(f32[11]{0:T(128)} %scale_hbm.1, f32[11,2048]{1,0:T(8,128)} %points_ref.1, f32[16,2048]{1,0:T(8,128)} %values_ref.1), custom_call_target="tpu_custom_call" | custom-call | tf_op jit(solution)/shard_map/matern/pallas_call | solution.py:306
  59.5 1.6 %copy.5 = f32[16,2048]{1,0:T(8,128)} copy(f32[16,2048]{1,0:T(8,128)} %matern.1) | data formatting | bytes 262144

commit v4 on v3

--- a/solution.py
+++ b/solution.py
@@ -61,7 +61,7 @@
     nc = pts // T
     own_steps = nc // 2 + 1
     total = own_steps + STEPS * nc
-    first = own_steps
+    first = own_steps - 2
     high_refs, low_refs = (kh0, kh1), (kl0, kl1)
 
     def ahead(d):
@@ -283,8 +283,6 @@
     final = place(jnp.int32(total - 1))
     for j in range(nc):
         apply(final, 0, j)
-
-    give_back(STEPS - 1)
 
     for k in range(STEPS):
         block_copy(send_buf, k, partner, 0).wait_send()

time: 61.2 us -> 61.7 us (level)
  no operation moved by 1% of the time
where the time goes in v4:
time: 61.7 us; the launch traced here: 61.6 us
  Pallas kernels  60 us (97%)
  local copies, waits for them, and re-layouts  1.57 us (3%)
    pallas_call x1, Pallas kernels, per_device(): pl.pallas_call(functools.partial(body, n), out_shape=jax.ShapeDtypeStruct...  60 us
    unnamed x1, local copies, waits for them, and re-layouts  1.57 us

profile of v4, /device:TPU:1, one launch (start us, length us, event | category | flops | bytes accessed | tf_op | source)
XLA Modules:
  0.0 61.6 jit_solution(3920505208354949121)
XLA Ops:
  0.0 60.0 %matern.1 = f32[16,2048]{1,0:T(8,128)} custom-call(f32[11]{0:T(128)} %scale_hbm.1, f32[11,2048]{1,0:T(8,128)} %points_ref.1, f32[16,2048]{1,0:T(8,128)} %values_ref.1), custom_call_target="tpu_custom_call" | custom-call | tf_op jit(solution)/shard_map/matern/pallas_call | solution.py:304
  60.0 1.6 %copy.5 = f32[16,2048]{1,0:T(8,128)} copy(f32[16,2048]{1,0:T(8,128)} %matern.1) | data formatting | bytes 262144

commit v5 on v1

--- a/solution.py
+++ b/solution.py
@@ -279,24 +279,38 @@
         return carry
 
     lax.fori_loop(0, (total - 1) // 2, pair, 0)
-    final = place(jnp.int32(total - 1))
+    slot, offset, _ = place(jnp.int32(total - 1))
+    last, last_slot = STEPS - 1, (STEPS - 1) % 2
     for j in range(nc):
-        apply(final, 0, j)
-
-    give_back(STEPS - 1)
-
+        tile, cols = slice(j * T, (j + 1) * T), column(j, offset)
+        oq[last_slot, :, cols] += dot(v_ref[OWN_SLOT, :, tile], kh0[:, tile])
+        oq8[last_slot, :, cols] += dot(v8_ref[OWN_SLOT, 0:16, tile], kl0[:, tile])
+    ret_send[last] = (
+        oq[last_slot, 0:16, :] + oq[last_slot, 16:32, :] + oq8[last_slot] * send_buf[feat + 2 : feat + 3, :]
+    )
+    return_copy(last).start()
+    for j in range(nc):
+        tile, cols = slice(j * T, (j + 1) * T), column(j, offset)
+        op[:, tile] += dot(v_ref[slot, :, cols], kh0[:, tile], True)
+        op8[:, tile] += dot(v8_ref[slot, 0:16, cols], kl0[:, tile], True)
+    for c in range(nc):
+        cols = slice(c * T, (c + 1) * T)
+        sums = op[:, cols] + oq[OWN_SLOT, :, cols]
+        low = op8[:, cols] * recv_buf[last, feat + 2 : feat + 3, cols]
+        own_low = oq8[OWN_SLOT, :, cols] * send_buf[feat + 2 : feat + 3, cols]
+        out_ref[:, cols] = sums[0:16] + sums[16:32] + low + own_low
+
+    for k in range(STEPS):
+        return_copy(k).wait_recv()
+    for c in range(nc):
+        cols = slice(c * T, (c + 1) * T)
+        result = out_ref[:, cols]
+        for k in range(STEPS):
+            result = result + ret_recv[k, :, cols]
+        out_ref[:, cols] = result
     for k in range(STEPS):
         block_copy(send_buf, k, partner, 0).wait_send()
         return_copy(k).wait_send()
-        return_copy(k).wait_recv()
-    for c in range(nc):
-        cols = slice(c * T, (c + 1) * T)
-        low = op8[:, cols] + oq8[OWN_SLOT, :, cols]
-        sums = op[:, cols] + oq[OWN_SLOT, :, cols]
-        result = sums[0:16] + sums[16:32] + low * send_buf[feat + 2 : feat + 3, cols]
-        for k in range(STEPS):
-            result = result + ret_recv[k, :, cols]
-        out_ref[:, cols] = result
 
 
 def per_device(n, points, values, inverse_scale):

time: 61.2 us -> 60.8 us (level)
  no operation moved by 1% of the time
where the time goes in v5:
time: 60.8 us; the launch traced here: 60.6 us
  Pallas kernels  57.5 us (95%)
  local copies, waits for them, and re-layouts  3.12 us (5%)
    pallas_call x1, Pallas kernels, per_device(): pl.pallas_call(functools.partial(body, n), out_shape=jax.ShapeDtypeStruct...  57.5 us
    unnamed x7, local copies, waits for them, and re-layouts  3.12 us

profile of v5, /device:TPU:1, one launch (start us, length us, event | category | flops | bytes accessed | tf_op | source)
XLA Modules:
  0.0 60.6 jit_solution(12146188655847137598)
XLA Ops:
  0.0 0.0 copy-start
  0.0 0.9 %copy-done = f32[11,2048]{1,0:T(8,128)S(1)} copy-done((f32[11,2048]{1,0:T(8,128)S(1)}, f32[11,2048]{1,0:T(8,128)}, u32[]{:S(2)}) %copy-start) | copy-done | bytes 90136
  0.9 0.0 copy-start.1
  0.9 0.9 %copy-done.1 = f32[16,2048]{1,0:T(8,128)S(1)} copy-done((f32[16,2048]{1,0:T(8,128)S(1)}, f32[16,2048]{1,0:T(8,128)}, u32[]{:S(2)}) %copy-start.1) | copy-done | bytes 131096
  1.8 0.0 copy-start.2
  1.8 0.7 %copy-done.2 = f32[11]{0:T(128)S(1)} copy-done((f32[11]{0:T(128)S(1)}, f32[11]{0:T(128)}, u32[]{:S(2)}) %copy-start.2) | copy-done | bytes 68
  2.5 57.5 %matern.1 = f32[16,2048]{1,0:T(8,128)S(1)} custom-call(f32[11]{0:T(128)S(1)} %copy-done.2, f32[11,2048]{1,0:T(8,128)S(1)} %copy-done, f32[16,2048]{1,0:T(8,128)S(1)} %copy-done.1), custom_call_target="tpu_custom_call" | custom-call | tf_op jit(solution)/shard_map/matern/pallas_call | solution.py:319
  60.0 0.7 %copy.5 = f32[16,2048]{1,0:T(8,128)} copy(f32[16,2048]{1,0:T(8,128)S(1)} %matern.1) | data formatting | bytes 262144
Async XLA Ops:
  0.0 0.9 %copy-start = (f32[11,2048]{1,0:T(8,128)S(1)}, f32[11,2048]{1,0:T(8,128)}, u32[]{:S(2)}) copy-start(f32[11,2048]{1,0:T(8,128)} %points_ref.1) | copy-start | bytes 270340
  0.9 0.9 %copy-start.1 = (f32[16,2048]{1,0:T(8,128)S(1)}, f32[16,2048]{1,0:T(8,128)}, u32[]{:S(2)}) copy-start(f32[16,2048]{1,0:T(8,128)} %values_ref.1) | copy-start | bytes 393220
  1.8 0.7 %copy-start.2 = (f32[11]{0:T(128)S(1)}, f32[11]{0:T(128)}, u32[]{:S(2)}) copy-start(f32[11]{0:T(128)} %scale_ref.1) | copy-start | bytes 136

commit v6 on v5

--- a/solution.py
+++ b/solution.py
@@ -348,7 +348,7 @@
             pltpu.SemaphoreType.DMA((2,)),
         ],
         compiler_params=pltpu.CompilerParams(
-            collective_id=0, has_side_effects=True, vmem_limit_bytes=48 << 20
+            collective_id=0, has_side_effects=True, vmem_limit_bytes=63 << 20
         ),
         name="matern",
     )(inverse_scale, points, values)

time: 60.8 us -> 61.4 us (level)
  Pallas kernels: 57.5 us -> 59.7 us
  local copies, waits for them, and re-layouts: 3.12 us -> 1.57 us
    pallas_call x1, Pallas kernels: 57.5 us -> 59.7 us  [per_device(): pl.pallas_call(functools.partial(body, n), out_shape=jax.ShapeDtypeStruct...]
    unnamed x7 -> x1, local copies, waits for them, and re-layouts: 3.12 us -> 1.57 us
where the time goes in v6:
time: 61.4 us; the launch traced here: 61.3 us
  Pallas kernels  59.7 us (97%)
  local copies, waits for them, and re-layouts  1.57 us (3%)
    pallas_call x1, Pallas kernels, per_device(): pl.pallas_call(functools.partial(body, n), out_shape=jax.ShapeDtypeStruct...  59.7 us
    unnamed x1, local copies, waits for them, and re-layouts  1.57 us

profile of v6, /device:TPU:1, one launch (start us, length us, event | category | flops | bytes accessed | tf_op | source)
XLA Modules:
  0.0 61.3 jit_solution(11993948532750973097)
XLA Ops:
  0.0 59.7 %matern.1 = f32[16,2048]{1,0:T(8,128)} custom-call(f32[11]{0:T(128)} %scale_ref.1, f32[11,2048]{1,0:T(8,128)} %points_ref.1, f32[16,2048]{1,0:T(8,128)} %values_ref.1), custom_call_target="tpu_custom_call" | custom-call | tf_op jit(solution)/shard_map/matern/pallas_call | solution.py:319
  59.8 1.6 %copy.5 = f32[16,2048]{1,0:T(8,128)} copy(f32[16,2048]{1,0:T(8,128)} %matern.1) | data formatting | bytes 262144
